TPU v7x, 32 devices: a whole 2x2x4 slice. The times are simulated.
32 devices in a mesh: groups: 2 (over y), dp: 4 (over z), mp: 2 (over x), pipe: 2 (over core).
Axes of the slice: x: 2, y: 2, z: 4, core: 2. Of those that a mesh axis runs over, the one named last changes fastest.
Arguments:
- tokens: bfloat16 [16384, 4608], P(('groups', 'dp', 'pipe'), 'mp'), parts along dimension 0, may hold values from -6 to 6
- cotangent: bfloat16 [16384, 2048], P(('groups', 'dp', 'pipe'), 'mp'), parts along dimension 0, may hold values from -0.15625 to 0.15625
- tok_job: int32 [16384], P(('groups', 'dp', 'pipe')), parts along dimension 0, may hold values from 0 to 3, as said below
- job_list: int32 [8, 2, 2], P('groups'), parts along dimension 0, may hold values from 0 to 3, as said below
- job_rank: int32 [8], P('groups'), parts along dimension 0, may hold values from 16 to 128, as said below
- adapter_a: bfloat16 [8, 128, 4608], P('groups', 'dp', 'mp'), parts along dimension 0, may hold values from -0.09375 to 0.09375
- adapter_b: bfloat16 [8, 128, 2048], P('groups', 'dp', 'mp'), parts along dimension 0, may hold values from -0.5 to 0.5
Outputs:
- adapted: bfloat16 [16384, 2048], P(('groups', 'dp', 'pipe'), 'mp'), parts along dimension 0
- grad_a: float32 [8, 128, 4608], P('groups', ('dp', 'pipe'), 'mp'), parts along dimension 0
- grad_b: float32 [8, 128, 2048], P('groups', ('dp', 'pipe'), 'mp'), parts along dimension 0
There are 2 independent parts, one for each index of `groups`. A program takes and returns all parts, laid end to end along the dimension named above; each array names one. Nothing has to cross between parts.
Inputs may be any that keep to these rules, and one draw needn't show every extreme that they name: `tok_job`: the tokens of device block b, rows b * 1024 to (b + 1) * 1024 - 1 with b = dp index * 2 + pipe index, have jobs from that device's entry of job_list. `job_list`: each device's 2 jobs are distinct. `job_rank`: every rank is a multiple of 16.
All inputs are finite; a program needn't handle non-finite values.
Results may differ from a plain program's by a relative error of at most 0.005.
Values may be sent and summed in bfloat16 or wider, within the bound.
A program may use at most 64 MiB of HBM per device.

v0:
```python
import jax
import jax.numpy as jnp
from jax import lax
from jax.sharding import PartitionSpec as P


def on_device(tokens, cotangent, tok_job, job_list, job_rank, adapter_a, adapter_b):
    high = lax.Precision.HIGHEST
    here = lax.axis_index("dp")
    layer = lax.axis_index("pipe")
    count_dp = lax.axis_size("dp")
    rank_full = adapter_a.shape[1] * count_dp
    slots = job_list.shape[2]
    adapters = adapter_a.shape[0]
    width_a = adapter_a.shape[2]
    width_b = adapter_b.shape[2]
    count = tokens.shape[0]
    peer_jobs = lax.dynamic_index_in_dim(job_list, layer, 1, keepdims=False)
    own_jobs = lax.dynamic_index_in_dim(peer_jobs, here, 0, keepdims=False)
    whole_a, whole_b = (
        lax.all_gather(adapter_a, "dp", axis=1, tiled=True),
        lax.all_gather(adapter_b, "dp", axis=1, tiled=True),
    )
    tiles_a = whole_a[own_jobs]
    tiles_b = whole_b[own_jobs]
    onehot = (tok_job[:, None] == own_jobs[None, :]).astype(jnp.float32)
    slot_ranks = job_rank[own_jobs]
    levels = lax.broadcasted_iota(jnp.int32, (slots, rank_full), 1)
    slot_mask = (levels < slot_ranks[:, None]).astype(jnp.float32)
    slot_scale = 8.0 / jnp.sqrt(slot_ranks.astype(jnp.float32))
    tok_mask = jnp.dot(onehot, slot_mask, precision=high)
    tok_scale = jnp.dot(onehot, slot_scale, precision=high)
    flat_a = tiles_a.reshape(slots * rank_full, width_a)
    flat_b = tiles_b.reshape(slots * rank_full, width_b)
    low_all = jnp.einsum("td,kd->tk", tokens, flat_a, preferred_element_type=jnp.float32)
    back_all = jnp.einsum("to,ko->tk", cotangent, flat_b, preferred_element_type=jnp.float32)
    low_part = jnp.sum(onehot[:, :, None] * low_all.reshape(count, slots, rank_full), axis=1)
    back_part = jnp.sum(onehot[:, :, None] * back_all.reshape(count, slots, rank_full), axis=1)
    low, back = lax.psum((low_part, back_part), "mp")
    scaled_low = (low * tok_mask * tok_scale[:, None]).astype(jnp.bfloat16)
    scaled_back = (back * tok_mask * tok_scale[:, None]).astype(jnp.bfloat16)
    picker = onehot.astype(jnp.bfloat16)[:, :, None]
    spread_low = (picker * scaled_low[:, None, :]).reshape(count, slots * rank_full)
    spread_back = (picker * scaled_back[:, None, :]).reshape(count, slots * rank_full)
    adapted = jnp.dot(spread_low, flat_b, preferred_element_type=jnp.float32).astype(jnp.bfloat16)
    part_b = jnp.einsum("tk,to->ko", spread_low, cotangent, preferred_element_type=jnp.float32)
    part_a = jnp.einsum("tk,td->kd", spread_back, tokens, preferred_element_type=jnp.float32)
    part_b = part_b.reshape(slots, rank_full, width_b)
    part_a = part_a.reshape(slots, rank_full, width_a)
    everyone = lax.broadcasted_iota(jnp.int32, (1, adapters), 1)
    select = (own_jobs[:, None] == everyone).astype(jnp.float32)
    dense_a = jnp.einsum("ja,jrd->ard", select, part_a, precision=high)
    dense_b = jnp.einsum("ja,jro->aro", select, part_b, precision=high)
    grad_a, grad_b = (
        lax.psum_scatter(dense_a, ("dp", "pipe"), scatter_dimension=1, tiled=True),
        lax.psum_scatter(dense_b, ("dp", "pipe"), scatter_dimension=1, tiled=True),
    )
    return (adapted, grad_a, grad_b)


def solution(mesh):
    in_specs = (
        P(("groups", "dp", "pipe"), "mp"),
        P(("groups", "dp", "pipe"), "mp"),
        P(("groups", "dp", "pipe")),
        P("groups", None, None),
        P("groups"),
        P("groups", "dp", "mp"),
        P("groups", "dp", "mp"),
    )
    out_specs = (
        P(("groups", "dp", "pipe"), "mp"),
        P("groups", ("dp", "pipe"), "mp"),
        P("groups", ("dp", "pipe"), "mp"),
    )
    return jax.shard_map(
        on_device, mesh=mesh, in_specs=in_specs, out_specs=out_specs, check_vma=False
    )
```

profile of v0, /device:TPU:0, one launch (start us, length us, event | category | flops | bytes accessed | tf_op | source)
XLA Modules:
  0.0 317.8 jit_solution(5957210010589070022)
XLA Ops:
  7.2 0.0 copy-start
  7.2 0.0 all-gather.5.cloned.1.call-start
  7.2 0.7 all-gather.5.cloned.1.call-update
  7.9 0.0 all-gather.3.cloned.1.call-start
  8.0 0.7 all-gather.3.cloned.1.call-update
  8.7 0.0 all-reduce.9.cloned.1.call-start
  8.7 0.9 dynamic-slice_reduce_fusion
  9.6 0.8 fusion.37
  10.4 29.9 %all-gather.5.cloned.1.call-done = bf16[4,128,1024]{2,1,0:T(8,128)(2,1)} async-done(((bf16[4,32,1024]{2,1,0:T(8,128)(2,1)}), bf16[4,128,1024]{2,1,0:T(8,128)(2,1)}) %all-gather.5.cloned.1.call-update) | async-done | bytes 1048592 | tf_op jit(solution)/shard_map/all_gather | solution.py:22
  40.2 1.8 gather_fusion.2
  42.1 0.0 copy-done
  42.1 1.7 fusion.39
  43.8 48.0 %all-gather.3.cloned.1.call-done = bf16[4,128,2304]{2,1,0:T(8,128)(2,1)} async-done(((bf16[4,32,2304]{2,1,0:T(8,128)(2,1)}), bf16[4,128,2304]{2,1,0:T(8,128)(2,1)}) %all-gather.3.cloned.1.call-update) | async-done | bytes 2359312 | tf_op jit(solution)/shard_map/all_gather | solution.py:21
  91.8 3.3 %gather_fusion = bf16[2,128,2304]{2,1,0:T(8,128)(2,1)} fusion(bf16[4,128,2304]{2,1,0:T(8,128)(2,1)} %all-gather.3.cloned.1.call-done, s32[1024]{0:T(1024)S(1)} %pad_clamp_fusion), kind=kCustom, calls=%fused_computation | custom fusion | bytes 2359304 | tf_op jit(solution)/shard_map/gather | solution.py:24
  95.1 0.0 copy-start.2
  95.1 4.2 %fusion.38 = f32[256,1024]{1,0:T(8,128)S(1)} fusion(bf16[256,2304]{1,0:T(8,128)(2,1)} %bitcast.51, bf16[1024,2304]{1,0:T(8,128)(2,1)} %param.7), kind=kOutput, calls=%fused_computation.55 | convolution fusion | flops 1207959552 | bytes 6946816 | tf_op jit(solution)/shard_map/td,kd->tk/dot_general | solution.py:35
  99.3 0.0 copy-done.2
  99.3 1.1 multiply_reduce_fusion
  100.4 0.0 copy-start.1
  100.4 0.0 copy-start.3
  100.4 2.1 copy.17
  102.4 1.0 copy.20
  103.4 0.0 all-reduce.9.cloned.1.call-update
  103.4 0.0 all-reduce.7.cloned.1.call-start
  103.5 0.0 copy-done.1
  103.5 0.6 gather_fusion.1
  104.1 0.0 copy-done.3
  104.1 0.2 fusion.17
  104.3 38.3 %all-reduce.9.cloned.1.call-done = (f32[1024,128]{1,0:T(8,128)}, f32[1024,128]{1,0:T(8,128)}) async-done(((f32[1024,128]{1,0:T(8,128)}, f32[1024,128]{1,0:T(8,128)}), (f32[1024,128]{1,0:T(8,128)}, f32[1024,128]{1,0:T(8,128)})) %all-reduce.9.cloned.1.call-update) | async-done | bytes 1048592 | tf_op jit(solution)/shard_map/psum | solution.py:39
  142.7 1.6 multiply_convert_fusion
  144.3 0.1 copy.21
  144.5 3.7 %fusion = f32[2,128,2304]{2,1,0:T(8,128)S(1)} fusion(bf16[1024,2304]{1,0:T(8,128)(2,1)} %param.7, bf16[1024,128]{0,1:T(8,128)(2,1)S(1)} %copy.21, bf16[1024,2]{0,1:T(2,128)(2,1)S(1)} %get-tuple-element.20), kind=kOutput, calls=%fused_computation.3 | convolution fusion | flops 1208221696 | bytes 7344128 | tf_op jit(solution)/shard_map/tk,td->kd/dot_general | solution.py:47
  148.2 7.8 %fusion.2 = f32[4,128,2304]{2,0,1:T(4,128)} fusion(f32[2,128,2304]{2,1,0:T(8,128)S(1)} %fusion, s32[2]{0:T(128)S(1)} %dynamic-slice_reduce_fusion), kind=kOutput, calls=%fused_computation.6 | convolution fusion | flops 28311560 | bytes 7077896 | tf_op jit(solution)/shard_map/ja,jrd->ard/dot_general | solution.py:52
  156.0 0.1 copy.18
  156.2 0.7 fusion.4
  156.9 4.1 %fusion.6 = f32[4,128,1024]{2,0,1:T(4,128)} fusion(f32[2,128,1024]{2,1,0:T(8,128)S(1)} %fusion.4, s32[2]{0:T(128)S(1)} %dynamic-slice_reduce_fusion), kind=kOutput, calls=%fused_computation.10 | convolution fusion | flops 12582920 | bytes 3145736 | tf_op jit(solution)/shard_map/ja,jro->aro/dot_general | solution.py:53
  160.9 0.0 copy-start.4
  160.9 0.0 all-reduce.7.cloned.1.call-update
  161.0 0.6 copy-done.4
  161.6 0.6 dynamic-slice.2
  162.8 2.1 bitcast_convert_fusion
  164.9 142.5 %all-reduce.7.cloned.1.call-done = (f32[4,128,2304]{2,0,1:T(4,128)}, f32[4,128,1024]{2,0,1:T(4,128)}) async-done(((f32[4,128,2304]{2,0,1:T(4,128)}, f32[4,128,1024]{2,0,1:T(4,128)}), (f32[4,128,2304]{2,0,1:T(4,128)}, f32[4,128,1024]{2,0,1:T(4,128)})) %all-reduce.7.cloned.1.call-update) | async-done | bytes 6815760
  307.4 1.1 constant_dynamic-slice_fusion.1
  308.5 0.9 copy.24
  309.4 1.0 constant_dynamic-slice_fusion
  310.4 0.9 copy.25
  (2 shorter events, 0.0 us)
Async XLA Ops:
  7.2 34.9 %copy-start = (bf16[1024,1024]{1,0:T(8,128)(2,1)S(1)}, bf16[1024,1024]{1,0:T(8,128)(2,1)}, u32[]{:S(2)}) copy-start(bf16[1024,1024]{1,0:T(8,128)(2,1)} %param.8) | copy-start | bytes 6291460
  7.2 33.1 %all-gather.5.cloned.1.call-start = ((), (), s32[]{:S(2)}) async-start(), calls=%async_computation.1 | async-start | bytes 1310720 | tf_op jit(solution)/shard_map/all_gather | solution.py:22
  7.9 83.9 %all-gather.3.cloned.1.call-start = ((), (), s32[]{:S(2)}) async-start(), calls=%async_computation | async-start | bytes 2949120 | tf_op jit(solution)/shard_map/all_gather | solution.py:21
  8.7 134.0 %all-reduce.9.cloned.1.call-start = ((), (), s32[]{:S(2)}) async-start(), calls=%async_computation.3 | async-start | bytes 2097152 | tf_op jit(solution)/shard_map/psum | solution.py:39
  95.1 4.2 %copy-start.2 = (f32[256,1024]{1,0:T(8,128)S(1)}, f32[256,1024]{1,0:T(8,128)}, u32[]{:S(2)}) copy-start(f32[256,1024]{1,0:T(8,128)} %fusion.39) | copy-start | bytes 3145732
  100.4 3.1 copy-start.1
  100.4 3.8 %copy-start.3 = (s32[1024]{0:T(1024)S(1)}, s32[1024]{0:T(1024)}, u32[]{:S(2)}) copy-start(s32[1024]{0:T(1024)} %param.9) | copy-start | bytes 12292
  103.4 204.0 %all-reduce.7.cloned.1.call-start = ((), (), s32[]{:S(2)}) async-start(), calls=%async_computation.2 | async-start | bytes 13631488
  160.9 0.7 copy-start.4
Sparse Core Ops, SparseCore 0:
  9.6 30.6 all-gather.4
  41.8 49.9 all-gather.2
  103.6 39.0 all-reduce.8
  161.1 146.2 all-reduce.6
where the time goes:
time: 318 us
  waiting for transfers between devices  260 us (82%)
  matrix products  26.1 us (8%)
  local copies, waits for them, and re-layouts  15 us (5%)
  between operations  14.5 us (5%)
    unnamed x5, waiting for transfers between devices  144 us
    all_gather x1, waiting for transfers between devices, on_device(): lax.all_gather(adapter_a, 'dp', axis=1, tiled=True)  48 us
    psum x1, waiting for transfers between devices, on_device(): low, back = lax.psum((low_part, back_part), 'mp')  38.3 us
    all_gather x1, waiting for transfers between devices, on_device(): lax.all_gather(adapter_b, 'dp', axis=1, tiled=True)  29.9 us
    dot_general x1, matrix products, on_device(): dense_a = jnp.einsum('ja,jrd->ard', select, part_a, precision=high)  7.82 us
  transfers between devices with their start and end apart: 4, of which 4 were waited for; matrix products, arithmetic and copies ran while one was open for 3% of the time, Pallas kernels for 0%

commit v1 on v0

--- a/solution.py
+++ b/solution.py
@@ -1,10 +1,333 @@
+import functools
+
 import jax
 import jax.numpy as jnp
 from jax import lax
+from jax.experimental import pallas as pl
+from jax.experimental.pallas import tpu as pltpu
 from jax.sharding import PartitionSpec as P
 
-
-def on_device(tokens, cotangent, tok_job, job_list, job_rank, adapter_a, adapter_b):
+TILE = 256
+ROWS16 = 16
+MESH = pl.DeviceIdType.MESH
+NT = (((1,), (1,)), ((), ()))
+TN = (((0,), (0,)), ((), ()))
+
+
+def fused(n, pipes, mps,
+          tokens_hbm, cot_hbm, job_ref, list_ref, rank_ref, a_hbm, b_hbm,
+          adapted, grad_a, grad_b,
+          tokens, cot, all_a, all_b, own, away, here_mp, spread, flat_b,
+          part_a, part_b, got_a, got_b,
+          local_sem, right_sem, left_sem, line_sem, sib_send, sib_recv,
+          mp_send, mp_recv, rs_send, rs_recv):
+    z = lax.axis_index("dp")
+    core = lax.axis_index("pipe")
+    lane = lax.axis_index("mp")
+    me = z * pipes + core
+    adapters, slots_here = a_hbm.shape[0], a_hbm.shape[1]
+    count = tokens.shape[0]
+    rank_full = n * slots_here
+    half = adapters // pipes
+    team = n * pipes
+
+    loads = [
+        pltpu.make_async_copy(b_hbm, all_b.at[z], local_sem.at[0]),
+        pltpu.make_async_copy(cot_hbm, cot, local_sem.at[1]),
+        pltpu.make_async_copy(a_hbm, all_a.at[z], local_sem.at[2]),
+        pltpu.make_async_copy(tokens_hbm, tokens, local_sem.at[3]),
+    ]
+    for load in loads:
+        load.start()
+
+    barrier = pltpu.get_barrier_semaphore()
+    for step in range(1, team):
+        peer = lax.rem(me + step, team)
+        pl.semaphore_signal(barrier, inc=1, device_id={"dp": peer // pipes, "pipe": lax.rem(peer, pipes)}, device_id_type=MESH)
+    for step in range(1, mps):
+        pl.semaphore_signal(barrier, inc=1, device_id={"mp": lax.rem(lane + step, mps)}, device_id_type=MESH)
+    pl.semaphore_wait(barrier, team - 1 + mps - 1)
+
+    stores = (all_a, all_b)
+    sources = (a_hbm, b_hbm)
+
+    def part_of(ref, c):
+        return ref.at[pl.ds(c * half, half)]
+
+    def line_copy(which, shard, rightward, first):
+        held = stores[which]
+        src = part_of(sources[which], core) if first else part_of(held.at[shard], core)
+        sem = right_sem if rightward else left_sem
+        return pltpu.make_async_remote_copy(
+            src_ref=src, dst_ref=part_of(held.at[shard], core),
+            send_sem=sem.at[which, shard], recv_sem=line_sem.at[which, shard],
+            device_id={"dp": z + 1 if rightward else z - 1}, device_id_type=MESH)
+
+    def sib_copy(which, shard, c):
+        held = stores[which]
+        return pltpu.make_async_remote_copy(
+            src_ref=part_of(held.at[shard], c), dst_ref=part_of(held.at[shard], c),
+            send_sem=sib_send.at[which, shard], recv_sem=sib_recv.at[which, shard],
+            device_id={"pipe": 1 - core}, device_id_type=MESH)
+
+    near = jnp.minimum(z, n - 1 - z)
+
+    def shard_at(i):
+        if i == 0:
+            return z
+        paired = z - (i + 1) // 2 if i % 2 else z + i // 2
+        return jnp.where(i <= 2 * near, paired, jnp.where(z < n - 1 - z, i, n - 1 - i))
+
+    def send_first(which):
+        @pl.when(z < n - 1)
+        def _():
+            line_copy(which, z, True, True).start()
+
+        @pl.when(z > 0)
+        def _():
+            line_copy(which, z, False, True).start()
+
+    def forward(which, i):
+        shard = shard_at(i)
+        line_copy(which, shard, True, False).wait_recv()
+
+        @pl.when(jnp.logical_and(shard < z, z < n - 1))
+        def _():
+            line_copy(which, shard, True, False).start()
+
+        @pl.when(jnp.logical_and(shard > z, z > 0))
+        def _():
+            line_copy(which, shard, False, False).start()
+
+        sib_copy(which, shard, core).start()
+
+    def finish_sends(which):
+        for i in range(n):
+            shard = shard_at(i)
+
+            @pl.when(jnp.logical_and(shard <= z, z < n - 1))
+            def _():
+                line_copy(which, shard, True, i == 0).wait_send()
+
+            @pl.when(jnp.logical_and(shard >= z, z > 0))
+            def _():
+                line_copy(which, shard, False, i == 0).wait_send()
+
+            if i > 0:
+                sib_copy(which, shard, core).wait_send()
+
+    def mp_copy(which, shard, step):
+        return pltpu.make_async_remote_copy(
+            src_ref=away.at[which, shard], dst_ref=here_mp.at[which, lane, shard],
+            send_sem=mp_send.at[which, shard, step], recv_sem=mp_recv.at[which, lane, shard],
+            device_id={"mp": lax.rem(lane + step, mps)}, device_id_type=MESH)
+
+    def mp_arrived(which, shard, step):
+        peer = lax.rem(lane + step, mps)
+        return pltpu.make_async_remote_copy(
+            src_ref=away.at[which, shard], dst_ref=here_mp.at[which, peer, shard],
+            send_sem=mp_send.at[which, shard, step], recv_sem=mp_recv.at[which, peer, shard],
+            device_id={"mp": peer}, device_id_type=MESH)
+
+    def project(which, i):
+        shard = shard_at(i)
+        held = stores[which]
+        rows = tokens if which == 0 else cot
+        if i > 0:
+            sib_copy(which, shard, 1 - core).wait_recv()
+        factor = held[shard].reshape(adapters * slots_here, held.shape[3])
+
+        @pl.loop(0, count // TILE)
+        def _(tile):
+            cols = pl.ds(pl.multiple_of(tile * TILE, TILE), TILE)
+            got = lax.dot_general(factor, rows[cols, :], NT, preferred_element_type=jnp.float32)
+            jobs = job_ref[:, cols]
+            value = jnp.zeros((slots_here, TILE), jnp.float32)
+            for a in range(adapters):
+                value = jnp.where(jobs == a, got[a * slots_here:(a + 1) * slots_here], value)
+            own[which, shard, :, cols] = value
+            away[which, shard, :, cols] = value.astype(jnp.bfloat16)
+
+        for step in range(1, mps):
+            mp_copy(which, shard, step).start()
+
+    first_job = list_ref[z, core, 0]
+    second_job = list_ref[z, core, 1]
+
+    def scale(which):
+        jobs = job_ref[...]
+        ranks = jnp.zeros_like(jobs)
+        for a in range(adapters):
+            ranks = jnp.where(jobs == a, rank_ref[a], ranks)
+        gain = 8.0 / jnp.sqrt(ranks.astype(jnp.float32))
+        for shard in range(n):
+            value = own[which, shard]
+            for step in range(1, mps):
+                mp_arrived(which, shard, step).wait_recv()
+                value = value + here_mp[which, lax.rem(lane + step, mps), shard].astype(jnp.float32)
+            level = lax.broadcasted_iota(jnp.int32, value.shape, 0) + shard * slots_here
+            value = jnp.where(level < ranks, value * gain, 0.0)
+            base = shard * slots_here
+            spread[which, base:base + slots_here, :] = jnp.where(jobs == first_job, value, 0.0).astype(jnp.bfloat16)
+            base += rank_full
+            spread[which, base:base + slots_here, :] = jnp.where(jobs == second_job, value, 0.0).astype(jnp.bfloat16)
+
+    def rs_copy(which, step):
+        dest = lax.rem(me + step, team)
+        part, got = ((part_a, got_a), (part_b, got_b))[which]
+        return pltpu.make_async_remote_copy(
+            src_ref=part.at[dest], dst_ref=got.at[me],
+            send_sem=rs_send.at[which, step], recv_sem=rs_recv.at[which, me],
+            device_id={"dp": dest // pipes, "pipe": lax.rem(dest, pipes)}, device_id_type=MESH)
+
+    def rs_arrived(which, step):
+        src = lax.rem(me + step, team)
+        part, got = ((part_a, got_a), (part_b, got_b))[which]
+        return pltpu.make_async_remote_copy(
+            src_ref=part.at[src], dst_ref=got.at[src],
+            send_sem=rs_send.at[which, step], recv_sem=rs_recv.at[which, src],
+            device_id={"dp": src // pipes, "pipe": lax.rem(src, pipes)}, device_id_type=MESH)
+
+    far_first = sorted(range(1, team), key=lambda step: abs(step - team // 2))
+
+    def gradient(which):
+        rows = tokens if which == 0 else cot
+        part, got = ((part_a, got_a), (part_b, got_b))[which]
+        weights = spread[1 - which]
+        each = rank_full // team
+
+        @pl.loop(0, rows.shape[1] // TILE)
+        def _(tile):
+            cols = pl.ds(pl.multiple_of(tile * TILE, TILE), TILE)
+            out = jnp.dot(weights, rows[:, cols], preferred_element_type=jnp.float32).astype(jnp.bfloat16)
+            for dest in range(team):
+                for slot in range(2):
+                    base = slot * rank_full + dest * each
+                    part[dest, slot, :, cols] = out[base:base + each]
+
+        for step in far_first:
+            rs_copy(which, step).start()
+        got[me] = part[me]
+
+    def collect(which):
+        part, got = ((part_a, got_a), (part_b, got_b))[which]
+        out = (grad_a, grad_b)[which]
+        for step in range(1, team):
+            rs_arrived(which, step).wait_recv()
+
+        @pl.loop(0, out.shape[2] // TILE)
+        def _(tile):
+            cols = pl.ds(pl.multiple_of(tile * TILE, TILE), TILE)
+            sums = [jnp.zeros((out.shape[1], TILE), jnp.float32) for _ in range(adapters)]
+            for src in range(team):
+                for slot in range(2):
+                    job = list_ref[src // pipes, src % pipes, slot]
+                    term = got[src, slot, :, cols].astype(jnp.float32)
+                    for a in range(adapters):
+                        sums[a] = sums[a] + term * jnp.where(job == a, 1.0, 0.0)
+            for a in range(adapters):
+                out[a, :, cols] = sums[a]
+
+    send_first(1)
+    send_first(0)
+    loads[0].wait()
+    loads[1].wait()
+    project(1, 0)
+    for i in range(1, n):
+        forward(1, i)
+        project(1, i)
+    loads[2].wait()
+    loads[3].wait()
+    forward(0, 1)
+    project(0, 0)
+    scale(1)
+    if n > 2:
+        forward(0, 2)
+    gradient(0)
+    project(0, 1)
+    for i in range(2, n):
+        if i > 2:
+            forward(0, i)
+        project(0, i)
+    for slot, job in enumerate((first_job, second_job)):
+        for shard in range(n):
+            base = slot * rank_full + shard * slots_here
+            flat_b[base:base + slots_here, :] = all_b[shard, job]
+    scale(0)
+    gradient(1)
+
+    @pl.loop(0, count // TILE)
+    def _(tile):
+        rows = pl.ds(pl.multiple_of(tile * TILE, TILE), TILE)
+        adapted[rows, :] = lax.dot_general(
+            spread[0, :, rows], flat_b[...], TN, preferred_element_type=jnp.float32).astype(jnp.bfloat16)
+
+    collect(0)
+    collect(1)
+    for which in range(2):
+        finish_sends(which)
+        for shard in range(n):
+            for step in range(1, mps):
+                mp_copy(which, shard, step).wait_send()
+        for step in range(1, team):
+            rs_copy(which, step).wait_send()
+
+
+def fits(mesh, tokens, cotangent, adapter_a, adapter_b):
+    n, pipes = mesh.shape["dp"], mesh.shape["pipe"]
+    slots = adapter_a.shape[1]
+    aligned = all(w % TILE == 0 for w in (tokens.shape[0], tokens.shape[1], cotangent.shape[1]))
+    return pipes == 2 and n >= 2 and n <= 8 and slots % (ROWS16 * pipes) == 0 and adapter_a.shape[0] % 2 == 0 and aligned
+
+
+def one_kernel(mesh, tokens, cotangent, tok_job, job_list, job_rank, adapter_a, adapter_b):
+    n, pipes, mps = mesh.shape["dp"], mesh.shape["pipe"], mesh.shape["mp"]
+    adapters, slots, width_a = adapter_a.shape
+    width_b = adapter_b.shape[2]
+    count = tokens.shape[0]
+    team = n * pipes
+    each = slots // pipes
+    bf16, f32 = jnp.bfloat16, jnp.float32
+    anywhere = pl.BlockSpec(memory_space=pl.ANY)
+    vmem = pl.BlockSpec(memory_space=pltpu.VMEM)
+    smem = pl.BlockSpec(memory_space=pltpu.SMEM)
+    dma = pltpu.SemaphoreType.DMA
+    return pl.pallas_call(
+        functools.partial(fused, n, pipes, mps),
+        out_shape=(
+            jax.ShapeDtypeStruct((count, width_b), bf16),
+            jax.ShapeDtypeStruct((adapters, each, width_a), f32),
+            jax.ShapeDtypeStruct((adapters, each, width_b), f32),
+        ),
+        in_specs=[anywhere, anywhere, vmem, smem, smem, anywhere, anywhere],
+        out_specs=(vmem, vmem, vmem),
+        scratch_shapes=[
+            pltpu.VMEM((count, width_a), bf16),
+            pltpu.VMEM((count, width_b), bf16),
+            pltpu.VMEM((n, adapters, slots, width_a), bf16),
+            pltpu.VMEM((n, adapters, slots, width_b), bf16),
+            pltpu.VMEM((2, n, slots, count), f32),
+            pltpu.VMEM((2, n, slots, count), bf16),
+            pltpu.VMEM((2, mps, n, slots, count), bf16),
+            pltpu.VMEM((2, 2 * n * slots, count), bf16),
+            pltpu.VMEM((2 * n * slots, width_b), bf16),
+            pltpu.VMEM((team, 2, each, width_a), bf16),
+            pltpu.VMEM((team, 2, each, width_b), bf16),
+            pltpu.VMEM((team, 2, each, width_a), bf16),
+            pltpu.VMEM((team, 2, each, width_b), bf16),
+            dma((4,)),
+            dma((2, n)), dma((2, n)), dma((2, n)), dma((2, n)), dma((2, n)),
+            dma((2, n, mps)), dma((2, mps, n)),
+            dma((2, team)), dma((2, team)),
+        ],
+        compiler_params=pltpu.CompilerParams(
+            collective_id=0, has_side_effects=True, vmem_limit_bytes=48 * 1024 * 1024),
+        cost_estimate=pl.CostEstimate(
+            flops=2 * count * 8 * n * slots * (width_a + width_b), bytes_accessed=12 * 1024 * 1024, transcendentals=0),
+    )(tokens, cotangent, tok_job.reshape(1, count), job_list, job_rank, adapter_a, adapter_b)
+
+
+def on_device_plain(tokens, cotangent, tok_job, job_list, job_rank, adapter_a, adapter_b):
     high = lax.Precision.HIGHEST
     here = lax.axis_index("dp")
     layer = lax.axis_index("pipe")
@@ -73,6 +396,12 @@
         P("groups", ("dp", "pipe"), "mp"),
         P("groups", ("dp", "pipe"), "mp"),
     )
+    def on_device(tokens, cotangent, tok_job, job_list, job_rank, adapter_a, adapter_b):
+        args = (tokens, cotangent, tok_job, job_list, job_rank, adapter_a, adapter_b)
+        if fits(mesh, tokens, cotangent, adapter_a, adapter_b):
+            return one_kernel(mesh, *args)
+        return on_device_plain(*args)
+
     return jax.shard_map(
         on_device, mesh=mesh, in_specs=in_specs, out_specs=out_specs, check_vma=False
     )

time: 318 us -> 85.5 us (0.27)
  waiting for transfers between devices: 260 us -> 0 us
  Pallas kernels: 0 us -> 76 us
  matrix products: 26.1 us -> 0 us
  between operations: 14.5 us -> 0.64 us
  local copies, waits for them, and re-layouts: 15 us -> 8.56 us
    unnamed x5 -> x0, waiting for transfers between devices: 144 us -> none
    all_gather x2 -> x0, waiting for transfers between devices: 77.9 us -> none  [the longest x1 48 us: on_device(): lax.all_gather(adapter_a, 'dp', axis=1, tiled=True)]
    pallas_call x0 -> x1, Pallas kernels: none -> 76 us  [one_kernel(): pl.pallas_call(functools.partial(fused, n, pipes, mps), out_shape=(jax.Sh...]
    psum x1 -> x0, waiting for transfers between devices: 38.3 us -> none  [on_device(): low, back = lax.psum((low_part, back_part), 'mp')]
    dot_general x9 -> x0, matrix products: 26.1 us -> none  [the longest x1 7.82 us: on_device(): dense_a = jnp.einsum('ja,jrd->ard', select, part_a, precision=high)]
    gather x3 -> x0, local copies, waits for them, and re-layouts: 5.74 us -> none  [the longest x1 3.3 us: on_device(): tiles_a = whole_a[own_jobs]]
    unnamed x15 -> x14, local copies, waits for them, and re-layouts: 5.08 us -> 8.56 us
  transfers between devices with their start and end apart: 4 -> 0, of which waited for: 4 -> 0; matrix products, arithmetic and copies ran while one was open for 3% -> 0% of each run, Pallas kernels for 0% -> 0%
where the time goes in v1:
time: 85.5 us; the launch traced here: 85.2 us
  Pallas kernels  76 us (89%)
  local copies, waits for them, and re-layouts  8.56 us (10%)
    pallas_call x1, Pallas kernels, one_kernel(): pl.pallas_call(functools.partial(fused, n, pipes, mps), out_shape=(jax.Sh...  76 us
    unnamed x14, local copies, waits for them, and re-layouts  8.56 us

profile of v1, /device:TPU:0, one launch (start us, length us, event | category | flops | bytes accessed | tf_op | source)
XLA Modules:
  0.0 85.2 jit_solution(4488926697510295662)
XLA Ops:
  0.6 0.8 copy.10.list_ref
  1.4 0.0 copy-start
  1.4 1.6 %copy-done = bf16[1024,1024]{1,0:T(8,128)(2,1)S(1)} copy-done((bf16[1024,1024]{1,0:T(8,128)(2,1)S(1)}, bf16[1024,1024]{1,0:T(8,128)(2,1)}, u32[]{:S(2)}) %copy-start) | copy-done | bytes 2097176
  3.0 0.0 copy-start.1
  3.0 1.1 %copy-done.1 = bf16[4,32,2304]{2,1,0:T(8,128)(2,1)S(1)} copy-done((bf16[4,32,2304]{2,1,0:T(8,128)(2,1)S(1)}, bf16[4,32,2304]{2,1,0:T(8,128)(2,1)}, u32[]{:S(2)}) %copy-start.1) | copy-done | bytes 589848
  4.1 0.0 copy-start.2
  4.1 0.9 %copy-done.2 = bf16[4,32,1024]{2,1,0:T(8,128)(2,1)S(1)} copy-done((bf16[4,32,1024]{2,1,0:T(8,128)(2,1)S(1)}, bf16[4,32,1024]{2,1,0:T(8,128)(2,1)}, u32[]{:S(2)}) %copy-start.2) | copy-done | bytes 262168
  5.0 0.0 copy-start.3
  5.0 0.7 copy-done.3
  5.7 0.0 copy-start.4
  5.7 0.7 copy-done.4
  6.4 76.0 %shard_map.94 = (bf16[1024,1024]{1,0:T(8,128)(2,1)S(1)}, f32[4,16,2304]{2,1,0:T(8,128)S(1)}, f32[4,16,1024]{2,1,0:T(8,128)S(1)}) custom-call(bf16[1024,2304]{1,0:T(8,128)(2,1)} %tokens_hbm.1, bf16[1024,1024]{1,0:T(8,128)(2,1)S(1)} %copy-done, s32[1,1024]{1,0:T(1,128)S(1)} %bitcast.1, s32[4,2,2]{2,1,0:T(2,128)S(1)} %copy.10.list_ref, s32[4]{0:T(128)S(1)} %copy-done.4, ...), custom_call_target="tpu_custom_call" | custom-call | flops 6979321856 | bytes 12582912 | tf_op jit(solution)/shard_map/pallas_call | solution.py:295
  82.3 1.3 %copy.14 = bf16[1024,1024]{1,0:T(8,128)(2,1)} copy(bf16[1024,1024]{1,0:T(8,128)(2,1)S(1)} %get-tuple-element.6) | data formatting | bytes 4194304
  83.7 0.8 copy.15
  84.5 0.7 copy.16
Async XLA Ops:
  1.4 1.6 %copy-start = (bf16[1024,1024]{1,0:T(8,128)(2,1)S(1)}, bf16[1024,1024]{1,0:T(8,128)(2,1)}, u32[]{:S(2)}) copy-start(bf16[1024,1024]{1,0:T(8,128)(2,1)} %cot_hbm.1) | copy-start | bytes 6291460
  3.0 1.1 %copy-start.1 = (bf16[4,32,2304]{2,1,0:T(8,128)(2,1)S(1)}, bf16[4,32,2304]{2,1,0:T(8,128)(2,1)}, u32[]{:S(2)}) copy-start(bf16[4,32,2304]{2,1,0:T(8,128)(2,1)} %a_hbm.1) | copy-start | bytes 1769476
  4.1 0.9 %copy-start.2 = (bf16[4,32,1024]{2,1,0:T(8,128)(2,1)S(1)}, bf16[4,32,1024]{2,1,0:T(8,128)(2,1)}, u32[]{:S(2)}) copy-start(bf16[4,32,1024]{2,1,0:T(8,128)(2,1)} %b_hbm.1) | copy-start | bytes 786436
  5.0 0.7 copy-start.3
  5.7 0.7 copy-start.4

commit v2 on v1

--- a/solution.py
+++ b/solution.py
@@ -18,9 +18,9 @@
           tokens_hbm, cot_hbm, job_ref, list_ref, rank_ref, a_hbm, b_hbm,
           adapted, grad_a, grad_b,
           tokens, cot, all_a, all_b, own, away, here_mp, spread, flat_b,
-          part_a, part_b, got_a, got_b,
+          part_a, part_b, got_a, got_b, mid_a, mid_b, dense_a, dense_b, far_a, far_b,
           local_sem, right_sem, left_sem, line_sem, sib_send, sib_recv,
-          mp_send, mp_recv, rs_send, rs_recv):
+          mp_send, mp_recv, rs_send, rs_recv, mid_recv, far_send, far_recv):
     z = lax.axis_index("dp")
     core = lax.axis_index("pipe")
     lane = lax.axis_index("mp")
@@ -172,27 +172,78 @@
             base += rank_full
             spread[which, base:base + slots_here, :] = jnp.where(jobs == second_job, value, 0.0).astype(jnp.bfloat16)
 
-    def rs_copy(which, step):
-        dest = lax.rem(me + step, team)
-        part, got = ((part_a, got_a), (part_b, got_b))[which]
-        return pltpu.make_async_remote_copy(
-            src_ref=part.at[dest], dst_ref=got.at[me],
-            send_sem=rs_send.at[which, step], recv_sem=rs_recv.at[which, me],
+    bridge = jnp.where(z < n // 2, n // 2 - 1, n // 2)
+    base_z = jnp.where(z < n // 2, 0, n // 2)
+    far_z = n // 2 - base_z
+    side = team // 2
+    spot = me - base_z * pipes
+
+    def parts_of(which):
+        return ((part_a, got_a, mid_a, dense_a, far_a), (part_b, got_b, mid_b, dense_b, far_b))[which]
+
+    def near_copy(which, source, target):
+        part, got = parts_of(which)[:2]
+        dest = base_z * pipes + target
+        return pltpu.make_async_remote_copy(
+            src_ref=part.at[dest], dst_ref=got.at[source],
+            send_sem=rs_send.at[which, dest], recv_sem=rs_recv.at[which, source],
             device_id={"dp": dest // pipes, "pipe": lax.rem(dest, pipes)}, device_id_type=MESH)
 
-    def rs_arrived(which, step):
-        src = lax.rem(me + step, team)
-        part, got = ((part_a, got_a), (part_b, got_b))[which]
-        return pltpu.make_async_remote_copy(
-            src_ref=part.at[src], dst_ref=got.at[src],
-            send_sem=rs_send.at[which, step], recv_sem=rs_recv.at[which, src],
-            device_id={"dp": src // pipes, "pipe": lax.rem(src, pipes)}, device_id_type=MESH)
-
-    far_first = sorted(range(1, team), key=lambda step: abs(step - team // 2))
+    def bridge_copy(which, source, far, c):
+        part, mid = parts_of(which)[0], parts_of(which)[2]
+        dest = (far_z + far) * pipes + c
+        return pltpu.make_async_remote_copy(
+            src_ref=part.at[dest], dst_ref=mid.at[source, far],
+            send_sem=rs_send.at[which, dest], recv_sem=mid_recv.at[which, source, far],
+            device_id={"dp": bridge, "pipe": c}, device_id_type=MESH)
+
+    def far_copy(which, far):
+        dense, landed = parts_of(which)[3:]
+        return pltpu.make_async_remote_copy(
+            src_ref=dense.at[far], dst_ref=landed,
+            send_sem=far_send.at[which, far], recv_sem=far_recv.at[which],
+            device_id={"dp": far_z + far}, device_id_type=MESH)
+
+    def each_bridge_send(which, act):
+        for far in range(n // 2):
+            for c in range(pipes):
+                @pl.when(jnp.logical_or(z != bridge, core != c))
+                def _():
+                    act(bridge_copy(which, spot, far, c))
+
+    def added(which, term_of, cols):
+        sums = [None] * adapters
+        for source in range(side):
+            for slot in range(2):
+                job = list_ref[base_z + source // pipes, source % pipes, slot]
+                term = term_of(source, slot, cols).astype(jnp.float32)
+                for a in range(adapters):
+                    piece = term * jnp.where(job == a, 1.0, 0.0)
+                    sums[a] = piece if sums[a] is None else sums[a] + piece
+        return sums
+
+    def combine(which):
+        part, _, mid, dense, _ = parts_of(which)
+
+        @pl.when(z == bridge)
+        def _():
+            for far in range(n // 2):
+                mid[spot, far] = part[(far_z + far) * pipes + core]
+                for step in range(1, side):
+                    bridge_copy(which, lax.rem(spot + step, side), far, core).wait_recv()
+
+                @pl.loop(0, dense.shape[3] // TILE)
+                def _(tile):
+                    cols = pl.ds(pl.multiple_of(tile * TILE, TILE), TILE)
+                    sums = added(which, lambda source, slot, cols: mid[source, far, slot, :, cols], cols)
+                    for a in range(adapters):
+                        dense[far, a, :, cols] = sums[a].astype(jnp.bfloat16)
+
+                far_copy(which, far).start()
 
     def gradient(which):
         rows = tokens if which == 0 else cot
-        part, got = ((part_a, got_a), (part_b, got_b))[which]
+        part, got = parts_of(which)[:2]
         weights = spread[1 - which]
         each = rank_full // team
 
@@ -205,28 +256,24 @@
                     base = slot * rank_full + dest * each
                     part[dest, slot, :, cols] = out[base:base + each]
 
-        for step in far_first:
-            rs_copy(which, step).start()
-        got[me] = part[me]
+        each_bridge_send(which, lambda copy: copy.start())
+        for step in range(1, side):
+            near_copy(which, spot, lax.rem(spot + step, side)).start()
+        got[spot] = part[me]
 
     def collect(which):
-        part, got = ((part_a, got_a), (part_b, got_b))[which]
+        got, landed = parts_of(which)[1], parts_of(which)[4]
         out = (grad_a, grad_b)[which]
-        for step in range(1, team):
-            rs_arrived(which, step).wait_recv()
+        for step in range(1, side):
+            near_copy(which, lax.rem(spot + step, side), spot).wait_recv()
+        far_copy(which, 0).wait_recv()
 
         @pl.loop(0, out.shape[2] // TILE)
         def _(tile):
             cols = pl.ds(pl.multiple_of(tile * TILE, TILE), TILE)
-            sums = [jnp.zeros((out.shape[1], TILE), jnp.float32) for _ in range(adapters)]
-            for src in range(team):
-                for slot in range(2):
-                    job = list_ref[src // pipes, src % pipes, slot]
-                    term = got[src, slot, :, cols].astype(jnp.float32)
-                    for a in range(adapters):
-                        sums[a] = sums[a] + term * jnp.where(job == a, 1.0, 0.0)
+            sums = added(which, lambda source, slot, cols: got[source, slot, :, cols], cols)
             for a in range(adapters):
-                out[a, :, cols] = sums[a]
+                out[a, :, cols] = sums[a] + landed[a, :, cols].astype(jnp.float32)
 
     send_first(1)
     send_first(0)
@@ -255,6 +302,7 @@
             flat_b[base:base + slots_here, :] = all_b[shard, job]
     scale(0)
     gradient(1)
+    combine(0)
 
     @pl.loop(0, count // TILE)
     def _(tile):
@@ -262,6 +310,7 @@
         adapted[rows, :] = lax.dot_general(
             spread[0, :, rows], flat_b[...], TN, preferred_element_type=jnp.float32).astype(jnp.bfloat16)
 
+    combine(1)
     collect(0)
     collect(1)
     for which in range(2):
@@ -269,15 +318,21 @@
         for shard in range(n):
             for step in range(1, mps):
                 mp_copy(which, shard, step).wait_send()
-        for step in range(1, team):
-            rs_copy(which, step).wait_send()
+        each_bridge_send(which, lambda copy: copy.wait_send())
+        for step in range(1, side):
+            near_copy(which, spot, lax.rem(spot + step, side)).wait_send()
+
+        @pl.when(z == bridge)
+        def _():
+            for far in range(n // 2):
+                far_copy(which, far).wait_send()
 
 
 def fits(mesh, tokens, cotangent, adapter_a, adapter_b):
     n, pipes = mesh.shape["dp"], mesh.shape["pipe"]
     slots = adapter_a.shape[1]
     aligned = all(w % TILE == 0 for w in (tokens.shape[0], tokens.shape[1], cotangent.shape[1]))
-    return pipes == 2 and n >= 2 and n <= 8 and slots % (ROWS16 * pipes) == 0 and adapter_a.shape[0] % 2 == 0 and aligned
+    return pipes == 2 and n >= 2 and n <= 8 and n % 2 == 0 and slots % (ROWS16 * pipes) == 0 and adapter_a.shape[0] % 2 == 0 and aligned
 
 
 def one_kernel(mesh, tokens, cotangent, tok_job, job_list, job_rank, adapter_a, adapter_b):
@@ -313,15 +368,22 @@
             pltpu.VMEM((2 * n * slots, width_b), bf16),
             pltpu.VMEM((team, 2, each, width_a), bf16),
             pltpu.VMEM((team, 2, each, width_b), bf16),
-            pltpu.VMEM((team, 2, each, width_a), bf16),
-            pltpu.VMEM((team, 2, each, width_b), bf16),
+            pltpu.VMEM((team // 2, 2, each, width_a), bf16),
+            pltpu.VMEM((team // 2, 2, each, width_b), bf16),
+            pltpu.VMEM((team // 2, n // 2, 2, each, width_a), bf16),
+            pltpu.VMEM((team // 2, n // 2, 2, each, width_b), bf16),
+            pltpu.VMEM((n // 2, adapters, each, width_a), bf16),
+            pltpu.VMEM((n // 2, adapters, each, width_b), bf16),
+            pltpu.VMEM((adapters, each, width_a), bf16),
+            pltpu.VMEM((adapters, each, width_b), bf16),
             dma((4,)),
             dma((2, n)), dma((2, n)), dma((2, n)), dma((2, n)), dma((2, n)),
             dma((2, n, mps)), dma((2, mps, n)),
-            dma((2, team)), dma((2, team)),
+            dma((2, team)), dma((2, team // 2)),
+            dma((2, team // 2, n // 2)), dma((2, n // 2)), dma((2,)),
         ],
         compiler_params=pltpu.CompilerParams(
-            collective_id=0, has_side_effects=True, vmem_limit_bytes=48 * 1024 * 1024),
+            collective_id=0, has_side_effects=True, vmem_limit_bytes=60 * 1024 * 1024),
         cost_estimate=pl.CostEstimate(
             flops=2 * count * 8 * n * slots * (width_a + width_b), bytes_accessed=12 * 1024 * 1024, transcendentals=0),
     )(tokens, cotangent, tok_job.reshape(1, count), job_list, job_rank, adapter_a, adapter_b)

time: 85.5 us -> 79.3 us (0.927)
  Pallas kernels: 76 us -> 71.6 us
  local copies, waits for them, and re-layouts: 8.56 us -> 6.04 us
    pallas_call x1, Pallas kernels: 76 us -> 71.6 us  [one_kernel(): pl.pallas_call(functools.partial(fused, n, pipes, mps), out_shape=(jax.Sh...]
    unnamed x14 -> x8, local copies, waits for them, and re-layouts: 8.56 us -> 6.04 us
where the time goes in v2:
time: 79.3 us; the launch traced here: 78.3 us
  Pallas kernels  71.6 us (90%)
  local copies, waits for them, and re-layouts  6.04 us (8%)
    pallas_call x1, Pallas kernels, one_kernel(): pl.pallas_call(functools.partial(fused, n, pipes, mps), out_shape=(jax.Sh...  71.6 us
    unnamed x8, local copies, waits for them, and re-layouts  6.04 us

profile of v2, /device:TPU:0, one launch (start us, length us, event | category | flops | bytes accessed | tf_op | source)
XLA Modules:
  0.0 78.3 jit_solution(14635406181872134145)
XLA Ops:
  0.6 1.4 %copy.10.list_ref = s32[4,2,2]{2,1,0:T(2,128)} copy(s32[4,2,2]{0,2,1:T(2,128)} %param.10) | data formatting | bytes 128 | tf_op args[3]
  2.0 71.6 %shard_map.94 = (bf16[1024,1024]{1,0:T(8,128)(2,1)}, f32[4,16,2304]{2,1,0:T(8,128)}, f32[4,16,1024]{2,1,0:T(8,128)}) custom-call(bf16[1024,2304]{1,0:T(8,128)(2,1)} %tokens_hbm.1, bf16[1024,1024]{1,0:T(8,128)(2,1)} %cot_hbm.1, s32[1,1024]{1,0:T(1,128)} %bitcast.1, s32[4,2,2]{2,1,0:T(2,128)} %copy.10.list_ref, s32[4]{0:T(128)} %rank_ref.1, ...), custom_call_target="tpu_custom_call" | custom-call | flops 6979321856 | bytes 12582912 | tf_op jit(solution)/shard_map/pallas_call | solution.py:350
  73.6 0.0 copy-start
  73.7 0.0 copy-start.1
  73.7 3.2 %copy.14 = bf16[1024,1024]{1,0:T(8,128)(2,1)} copy(bf16[1024,1024]{1,0:T(8,128)(2,1)} %get-tuple-element.6) | data formatting | bytes 4194304
  76.8 0.0 copy-done
  76.8 0.8 %copy.15 = f32[4,16,2304]{2,1,0:T(8,128)} copy(f32[4,16,2304]{2,1,0:T(8,128)S(1)} %copy-done) | data formatting | bytes 1179648
  77.6 0.0 copy-done.1
  77.6 0.7 copy.16
Async XLA Ops:
  73.6 3.2 %copy-start = (f32[4,16,2304]{2,1,0:T(8,128)S(1)}, f32[4,16,2304]{2,1,0:T(8,128)}, u32[]{:S(2)}) copy-start(f32[4,16,2304]{2,1,0:T(8,128)} %get-tuple-element.7) | copy-start | bytes 1769476
  73.7 4.0 %copy-start.1 = (f32[4,16,1024]{2,1,0:T(8,128)S(1)}, f32[4,16,1024]{2,1,0:T(8,128)}, u32[]{:S(2)}) copy-start(f32[4,16,1024]{2,1,0:T(8,128)} %get-tuple-element.8) | copy-start | bytes 786436

commit v3 on v2

--- a/solution.py
+++ b/solution.py
@@ -137,12 +137,12 @@
             sib_copy(which, shard, 1 - core).wait_recv()
         factor = held[shard].reshape(adapters * slots_here, held.shape[3])
 
-        @pl.loop(0, count // TILE)
+        @pl.loop(0, count // 512)
         def _(tile):
-            cols = pl.ds(pl.multiple_of(tile * TILE, TILE), TILE)
+            cols = pl.ds(pl.multiple_of(tile * 512, 512), 512)
             got = lax.dot_general(factor, rows[cols, :], NT, preferred_element_type=jnp.float32)
             jobs = job_ref[:, cols]
-            value = jnp.zeros((slots_here, TILE), jnp.float32)
+            value = jnp.zeros((slots_here, 512), jnp.float32)
             for a in range(adapters):
                 value = jnp.where(jobs == a, got[a * slots_here:(a + 1) * slots_here], value)
             own[which, shard, :, cols] = value

time: 79.3 us -> 78.5 us (0.990)
  no operation moved by 1% of the time
where the time goes in v3:
time: 78.5 us; the launch traced here: 77.7 us
  Pallas kernels  71 us (90%)
  local copies, waits for them, and re-layouts  6.04 us (8%)
    pallas_call x1, Pallas kernels, one_kernel(): pl.pallas_call(functools.partial(fused, n, pipes, mps), out_shape=(jax.Sh...  71 us
    unnamed x8, local copies, waits for them, and re-layouts  6.04 us

profile of v3, /device:TPU:0, one launch (start us, length us, event | category | flops | bytes accessed | tf_op | source)
XLA Modules:
  0.0 77.7 jit_solution(514535362146331538)
XLA Ops:
  0.6 1.4 %copy.10.list_ref = s32[4,2,2]{2,1,0:T(2,128)} copy(s32[4,2,2]{0,2,1:T(2,128)} %param.10) | data formatting | bytes 128 | tf_op args[3]
  2.0 71.0 %shard_map.94 = (bf16[1024,1024]{1,0:T(8,128)(2,1)}, f32[4,16,2304]{2,1,0:T(8,128)}, f32[4,16,1024]{2,1,0:T(8,128)}) custom-call(bf16[1024,2304]{1,0:T(8,128)(2,1)} %tokens_hbm.1, bf16[1024,1024]{1,0:T(8,128)(2,1)} %cot_hbm.1, s32[1,1024]{1,0:T(1,128)} %bitcast.1, s32[4,2,2]{2,1,0:T(2,128)} %copy.10.list_ref, s32[4]{0:T(128)} %rank_ref.1, ...), custom_call_target="tpu_custom_call" | custom-call | flops 6979321856 | bytes 12582912 | tf_op jit(solution)/shard_map/pallas_call | solution.py:350
  73.0 0.0 copy-start
  73.0 0.0 copy-start.1
  73.0 3.2 %copy.14 = bf16[1024,1024]{1,0:T(8,128)(2,1)} copy(bf16[1024,1024]{1,0:T(8,128)(2,1)} %get-tuple-element.6) | data formatting | bytes 4194304
  76.2 0.0 copy-done
  76.2 0.8 %copy.15 = f32[4,16,2304]{2,1,0:T(8,128)} copy(f32[4,16,2304]{2,1,0:T(8,128)S(1)} %copy-done) | data formatting | bytes 1179648
  77.0 0.0 copy-done.1
  77.0 0.7 copy.16
Async XLA Ops:
  73.0 3.2 %copy-start = (f32[4,16,2304]{2,1,0:T(8,128)S(1)}, f32[4,16,2304]{2,1,0:T(8,128)}, u32[]{:S(2)}) copy-start(f32[4,16,2304]{2,1,0:T(8,128)} %get-tuple-element.7) | copy-start | bytes 1769476
  73.0 4.0 %copy-start.1 = (f32[4,16,1024]{2,1,0:T(8,128)S(1)}, f32[4,16,1024]{2,1,0:T(8,128)}, u32[]{:S(2)}) copy-start(f32[4,16,1024]{2,1,0:T(8,128)} %get-tuple-element.8) | copy-start | bytes 786436
